TPU v7x, 32 devices: a whole 2x2x4 slice. The times are simulated.
32 devices in a mesh: dp: 4 (over y, x), shard: 8 (over z, core).
Axes of the slice: x: 2, y: 2, z: 4, core: 2. Of those that a mesh axis runs over, the one named last changes fastest.
Arguments:
- hot_ids: int32 [4096, 8], P(('dp', 'shard')), may hold values from 0 to 4095
- cold_owner: int32 [8192, 1], P(('dp', 'shard')), may hold values from 0 to 7; in each aligned block of 256 rows (0 to 255, 256 to 511, ...) at most 64 rows name the same one
- cold_offset: int32 [8192], P(('dp', 'shard')), may hold values from 0 to 4095
- hot_table: bfloat16 [4096, 128], replicated, may hold values from -2 to 2
- cold_table: bfloat16 [32768, 128], P('shard'), may hold values from -4 to 4
- w_in: bfloat16 [256, 4096], P(None, 'shard'), may hold values from -0.375 to 0.375
- bias_in: bfloat16 [1, 4096], P(None, 'shard'), may hold values from -0.59765625 to 0.59765625
- w_out: bfloat16 [1, 4096], P(None, 'shard'), may hold values from -0.1875 to 0.1875
- cotangent: float32 [4096], P(('dp', 'shard')), may hold values from -10 to 10
Outputs:
- logits: float32 [4096], P(('dp', 'shard'))
- hot_grad: bfloat16 [4096, 128], P('shard')
- cold_grad: bfloat16 [32768, 128], P('shard')
- w_in_grad: float32 [256, 4096], P(None, 'shard')
Inputs may be any that keep to these rules, and one draw needn't show every extreme that they name: `cold_owner`: within the 256 cold lookups of one device no owner is named more than 64 times, a bound that some block reaches.
All inputs are finite; a program needn't handle non-finite values.
Results may differ from a plain program's by a relative error of at most 0.015.
Values may be sent and summed in bfloat16 or wider, within the bound.
A program may use at most 64 MiB of HBM per device.

v0:
```python
import jax
import jax.numpy as jnp
from jax import lax
from jax.sharding import PartitionSpec as P


def contract_rows(left, right):
    return lax.dot_general(
        left, right, (((0,), (0,)), ((), ())), preferred_element_type=jnp.float32
    )


def shards(
    hot_ids, cold_owner, cold_offset, hot_table, cold_table, w_in, bias_in, w_out, cotangent
):
    shard_count = lax.axis_size("shard")
    my_index = lax.axis_index("shard")
    samples_dev = hot_ids.shape[0]
    hot_width = hot_ids.shape[1]
    table_rows = hot_table.shape[0]
    embed = hot_table.shape[1]
    kept_rows = table_rows // shard_count
    owned_rows = cold_table.shape[0]
    row_numbers = jnp.arange(table_rows, dtype=jnp.int32)
    hot_counts = jnp.zeros((samples_dev, table_rows), jnp.float32)
    for lookup in range(hot_width):
        hot_counts = hot_counts + (hot_ids[:, lookup][:, None] == row_numbers[None, :]).astype(
            jnp.float32
        )
    hot_counts = hot_counts.astype(jnp.bfloat16)
    hot_pooled = jnp.dot(hot_counts, hot_table, preferred_element_type=jnp.float32)
    owner_ids = cold_owner[:, 0]
    lookups = owner_ids.shape[0]
    per_sample = lookups // samples_dev
    capacity = max(2, 2 * lookups // shard_count)
    matches = (owner_ids[:, None] == jnp.arange(shard_count, dtype=jnp.int32)[None, :]).astype(
        jnp.int32
    )
    ordinal = jnp.cumsum(matches, axis=0) - 1
    slot_index = jnp.sum(ordinal * matches, axis=1)
    slot_place = owner_ids * capacity + slot_index
    slot_match = slot_place[:, None] == jnp.arange(shard_count * capacity, dtype=jnp.int32)[None, :]
    requests = jnp.sum(jnp.where(slot_match, cold_offset[:, None], 0), axis=0).reshape(
        shard_count, capacity
    )
    present = jnp.sum(slot_match.astype(jnp.int32), axis=0).reshape(shard_count, capacity)
    slot_table = slot_match.astype(jnp.bfloat16)
    offsets = lax.all_to_all(requests, "shard", split_axis=0, concat_axis=0, tiled=True)
    markers = lax.all_to_all(present, "shard", split_axis=0, concat_axis=0, tiled=True)
    fetched = jnp.take(cold_table, offsets, axis=0)
    fetched = jnp.where(markers[:, :, None] > 0, fetched, jnp.zeros_like(fetched))
    answer = lax.all_to_all(fetched, "shard", split_axis=0, concat_axis=0, tiled=True)
    mine = jnp.dot(slot_table, answer.reshape(-1, embed), preferred_element_type=jnp.float32)
    cold_pooled = jnp.sum(mine.reshape(samples_dev, per_sample, embed), axis=1)
    inputs = jnp.concatenate([hot_pooled, cold_pooled], axis=1).astype(jnp.bfloat16)
    group_inputs = lax.all_gather(inputs, "shard", axis=0, tiled=True)
    preact = (
        jnp.dot(group_inputs, w_in, preferred_element_type=jnp.float32)
        + bias_in[0].astype(jnp.float32)[None, :]
    )
    sigma = jax.nn.sigmoid(preact)
    hidden = (preact * sigma).astype(jnp.bfloat16)
    logit_share = jnp.dot(hidden, w_out[0], preferred_element_type=jnp.float32)
    group_logits = lax.psum(logit_share, "shard")
    logits = lax.dynamic_slice_in_dim(group_logits, my_index * samples_dev, samples_dev, 0)
    group_cotangent = lax.all_gather(cotangent, "shard", axis=0, tiled=True)
    slope = sigma * (1.0 + preact * (1.0 - sigma))
    hidden_grad = (group_cotangent[:, None] * w_out[0].astype(jnp.float32)[None, :] * slope).astype(
        jnp.bfloat16
    )
    weight_group = contract_rows(group_inputs, hidden_grad).astype(jnp.bfloat16)
    input_grad = lax.psum_scatter(
        jnp.dot(hidden_grad, w_in.T, preferred_element_type=jnp.float32).astype(jnp.bfloat16),
        "shard",
        scatter_dimension=0,
        tiled=True,
    )
    hot_part = contract_rows(hot_counts, input_grad[:, :embed])
    hot_everywhere = lax.psum(hot_part, ("dp", "shard"))
    hot_total = lax.dynamic_slice_in_dim(hot_everywhere, my_index * kept_rows, kept_rows, 0)
    per_lookup = jnp.repeat(input_grad[:, embed:], per_sample, axis=0)
    outgoing = (
        contract_rows(slot_table, per_lookup)
        .astype(jnp.bfloat16)
        .reshape(shard_count, capacity, embed)
    )
    incoming = lax.all_to_all(outgoing, "shard", split_axis=0, concat_axis=0, tiled=True)
    offset_table = (
        offsets.reshape(-1)[:, None] == jnp.arange(owned_rows, dtype=jnp.int32)[None, :]
    ).astype(jnp.bfloat16)
    cold_part = contract_rows(offset_table, incoming.reshape(-1, embed))
    cold_total, weight_total = (
        lax.psum(cold_part.astype(jnp.bfloat16), "dp").astype(jnp.float32),
        lax.psum(weight_group, "dp").astype(jnp.float32),
    )
    return (logits, hot_total.astype(jnp.bfloat16), cold_total.astype(jnp.bfloat16), weight_total)


def solution(mesh):
    in_specs = (
        P(("dp", "shard"), None),
        P(("dp", "shard"), None),
        P(("dp", "shard")),
        P(),
        P("shard", None),
        P(None, "shard"),
        P(None, "shard"),
        P(None, "shard"),
        P(("dp", "shard")),
    )
    out_specs = (P(("dp", "shard")), P("shard", None), P("shard", None), P(None, "shard"))
    return jax.shard_map(shards, mesh=mesh, in_specs=in_specs, out_specs=out_specs, check_vma=False)
```

profile of v0, /device:TPU:0, one launch (start us, length us, event | category | flops | bytes accessed | tf_op | source)
XLA Modules:
  0.0 214.7 jit_solution(14971163135114629105)
XLA Ops:
  7.2 0.0 copy-start
  7.2 0.8 fusion.11
  8.0 0.6 reduce-window.6
  8.5 0.2 slice_reduce_fusion
  8.8 0.8 fusion.10
  9.6 0.5 broadcast.99
  10.1 1.3 fusion.14
  11.4 0.8 convert_reduce_fusion
  12.3 0.7 all_to_all.24
  12.9 6.3 %all-to-all-start.1 = ((s32[8,1,64]{2,1,0:T(1,128)}), s32[8,1,64]{2,1,0:T(1,128)S(1)}, u32[]{:S(2)}, u32[]{:S(2)}) async-start(s32[8,1,64]{2,1,0:T(1,128)} %all_to_all.24), calls=%async_computation.1 | async-start | bytes 8192 | tf_op jit(solution)/shard_map/all_to_all | solution.py:48
  19.3 1.0 slice_bitcast_fusion.7
  20.2 0.7 reduce.2
  20.9 0.7 add.104
  21.6 0.7 all_to_all.22
  22.3 0.1 eq.239
  22.4 0.1 copy.20
  22.5 12.3 %all-gather = f32[8,1,128]{2,1,0:T(1,128)S(1)} all-gather(f32[1,1,128]{2,1,0:T(1,128)} %bitcast.77), channel_id=1, replica_groups=mesh['dp'=4,'shard'=8] {'shard'}, dimensions={0}, use_global_device_ids=true | all-gather | bytes 4608 | tf_op jit(solution)/shard_map/all_gather | solution.py:66
  34.8 0.0 all-to-all-done.1
  34.8 3.3 %all-to-all-start = ((s32[8,1,64]{2,1,0:T(1,128)}), s32[8,1,64]{2,1,0:T(1,128)S(1)}, u32[]{:S(2)}, u32[]{:S(2)}) async-start(s32[8,1,64]{2,1,0:T(1,128)} %all_to_all.22), calls=%async_computation | async-start | bytes 8192 | tf_op jit(solution)/shard_map/all_to_all | solution.py:49
  38.2 0.1 reshape.125
  38.3 5.3 %all-to-all-done = s32[8,1,64]{2,1,0:T(1,128)S(1)} async-done(((s32[8,1,64]{2,1,0:T(1,128)}), s32[8,1,64]{2,1,0:T(1,128)S(1)}, u32[]{:S(2)}, u32[]{:S(2)}) %all-to-all-start) | async-done | bytes 2080 | tf_op jit(solution)/shard_map/all_to_all | solution.py:49
  43.6 0.0 copy-done
  43.6 1.3 gather_fusion
  44.9 0.9 select_select_fusion
  45.8 3.4 %all-to-all-start.2 = ((bf16[8,64,128]{2,1,0:T(8,128)(2,1)}), bf16[8,64,128]{2,1,0:T(8,128)(2,1)S(1)}, u32[]{:S(2)}, u32[]{:S(2)}) async-start(bf16[8,64,128]{2,1,0:T(8,128)(2,1)} %select_select_fusion), calls=%async_computation.2 | async-start | bytes 262144 | tf_op jit(solution)/shard_map/all_to_all | solution.py:52
  49.2 0.0 reduce-scatter.2.cloned.1.call-start
  49.2 0.0 copy-start.1
  49.2 3.7 %convolution_convert_fusion.3 = bf16[128,128]{0,1:T(8,128)(2,1)S(1)} fusion(bf16[4096,128]{1,0:T(8,128)(2,1)} %param.12, s32[128]{0:T(128)S(1)} %get-tuple-element.16, s32[128]{0:T(128)S(1)} %get-tuple-element.17, s32[128]{0:T(128)S(1)} %get-tuple-element.11, s32[128]{0:T(128)S(1)} %get-tuple-element.12, s32[128]{0:T(128)S(1)} %get-tuple-element.13, ...), kind=kOutput, calls=%fused_computation.21 | convolution fusion | flops 146817024 | bytes 1085440 | tf_op jit(solution)/shard_map/dot_general | solution.py:31
  53.0 2.9 %all-to-all-done.2 = bf16[8,64,128]{2,1,0:T(8,128)(2,1)S(1)} async-done(((bf16[8,64,128]{2,1,0:T(8,128)(2,1)}), bf16[8,64,128]{2,1,0:T(8,128)(2,1)S(1)}, u32[]{:S(2)}, u32[]{:S(2)}) %all-to-all-start.2) | async-done | bytes 131104 | tf_op jit(solution)/shard_map/all_to_all | solution.py:52
  55.9 0.3 convolution_reduce_fusion
  56.1 0.1 copy.22
  56.3 14.0 %all_gather.6 = bf16[1024,256]{0,1:T(8,128)(2,1)S(1)} all-gather(bf16[128,256]{0,1:T(8,128)(2,1)S(1)} %pad_maximum_fusion), channel_id=1, replica_groups=mesh['dp'=4,'shard'=8] {'shard'}, dimensions={0}, use_global_device_ids=true | all-gather | bytes 589824 | tf_op jit(solution)/shard_map/all_gather | solution.py:56
  70.3 0.0 copy-done.1
  70.3 2.3 %multiply_convert_fusion = (bf16[1024,512]{1,0:T(8,128)(2,1)S(1)}, f32[1024,512]{1,0:T(8,128)}) fusion(f32[512]{0:T(512)S(1)} %mul.50, f32[1024]{0:T(1024)S(1)} %bitcast.70, f32[512]{0:T(512)S(1)} %bitcast.75, bf16[1024,256]{0,1:T(8,128)(2,1)S(1)} %all_gather.6, bf16[256,512]{1,0:T(8,128)(2,1)S(1)} %copy-done.1), kind=kOutput, calls=%fused_computation.5 | convolution fusion | flops 274202624 | bytes 3940352 | tf_op jit(solution)/shard_map/dot_general | solution.py:58
  72.6 1.3 convolution_convert_fusion
  73.9 0.0 reduce-scatter.2.cloned.1.call-update
  73.9 0.7 reduce.10
  74.5 0.1 eq.248
  74.6 28.9 %reduce-scatter.2.cloned.1.call-done = bf16[128,256]{1,0:T(8,128)(2,1)} async-done(((bf16[1024,256]{1,0:T(8,128)(2,1)}), bf16[128,256]{1,0:T(8,128)(2,1)}) %reduce-scatter.2.cloned.1.call-update) | async-done | bytes 65552 | tf_op jit(solution)/shard_map/reduce_scatter | solution.py:72
  103.5 0.8 slice.52
  104.3 1.1 convolution_convert_fusion.2
  105.4 3.4 %all-to-all-start.3 = ((bf16[8,64,128]{2,1,0:T(8,128)(2,1)}), bf16[8,64,128]{2,1,0:T(8,128)(2,1)S(1)}, u32[]{:S(2)}, u32[]{:S(2)}) async-start(bf16[8,64,128]{2,1,0:T(8,128)(2,1)} %bitcast.27), calls=%async_computation.4 | async-start | bytes 262144 | tf_op jit(solution)/shard_map/all_to_all | solution.py:87
  108.8 0.0 all-reduce.4.cloned.1.call-start
  108.8 1.2 convolution_convert_fusion.1
  110.0 5.5 %all-to-all-done.3 = bf16[8,64,128]{2,1,0:T(8,128)(2,1)S(1)} async-done(((bf16[8,64,128]{2,1,0:T(8,128)(2,1)}), bf16[8,64,128]{2,1,0:T(8,128)(2,1)S(1)}, u32[]{:S(2)}, u32[]{:S(2)}) %all-to-all-start.3) | async-done | bytes 131104 | tf_op jit(solution)/shard_map/all_to_all | solution.py:87
  115.5 0.0 copy-start.3
  115.5 3.4 %fusion.1 = bf16[4096,128]{1,0:T(8,128)(2,1)} fusion(bf16[512,128]{1,0:T(8,128)(2,1)S(1)} %bitcast.62, s32[512]{0:T(512)S(1)} %eq.248), kind=kOutput, calls=%fused_computation.3 | convolution fusion | flops 539492352 | bytes 1181696 | tf_op jit(solution)/shard_map/dot_general | solution.py:8
  118.9 0.0 all-reduce.4.cloned.1.call-update
  118.9 0.0 copy-done.3
  118.9 0.0 copy-start.2
  118.9 2.3 %fusion.3 = f32[1,1024]{1,0:T(1,128)S(1)} fusion(f32[1024,512]{1,0:T(8,128)} %get-tuple-element.19, f32[512]{0:T(512)S(1)} %bitcast.76, bf16[1,512]{1,0:T(2,128)(2,1)S(1)} %copy-done.3), kind=kOutput, calls=%fused_computation.22 | convolution fusion | flops 4194304 | bytes 2104320 | tf_op jit(solution)/shard_map/dot_general | solution.py:63
  121.2 14.4 %psum.28 = f32[1024]{0:T(1024)S(1)} all-reduce(f32[1024]{0:T(1024)S(1)} %bitcast.71), channel_id=1, replica_groups=mesh['dp'=4,'shard'=8] {'shard'}, use_global_device_ids=true, to_apply=%region_6.7 | all-reduce | flops 1024 | bytes 8192 | tf_op jit(solution)/shard_map/psum | solution.py:64
  135.6 0.6 dynamic_slice.6
  136.2 0.0 copy-done.2
  136.2 2.3 %fusion.6 = f32[4096,128]{1,0:T(8,128)S(1)} fusion(s32[128]{0:T(128)S(1)} %get-tuple-element.16, s32[128]{0:T(128)S(1)} %get-tuple-element.17, s32[128]{0:T(128)S(1)} %get-tuple-element.11, s32[128]{0:T(128)S(1)} %get-tuple-element.12, s32[128]{0:T(128)S(1)} %get-tuple-element.13, s32[128]{0:T(128)S(1)} %get-tuple-element.14, ...), kind=kOutput, calls=%fused_computation.28 | convolution fusion | flops 146800640 | bytes 2134016 | tf_op jit(solution)/shard_map/dot_general | solution.py:8
  138.6 63.7 %all-reduce.5 = bf16[4096,128]{1,0:T(8,128)(2,1)} all-reduce(f32[4096,128]{1,0:T(8,128)S(1)} %fusion.6), channel_id=1, replica_groups=mesh['dp'=4,'shard'=8] {'dp','shard'}, use_global_device_ids=true, to_apply=%region_8.9 | all-reduce | flops 524288 | bytes 3145728 | tf_op jit(solution)/shard_map/psum | solution.py:79
  202.3 1.6 dynamic-slice_convert_fusion
  203.8 0.0 all-reduce.4.cloned.1.call-done
  203.8 1.8 convert_element_type.86
  205.6 2.3 %copy.27 = bf16[4096,128]{1,0:T(8,128)(2,1)} copy(bf16[4096,128]{1,0:T(8,128)(2,1)} %get-tuple-element.22) | data formatting | bytes 2097152
  (9 shorter events, 0.1 us)
Async XLA Ops:
  7.2 36.4 %copy-start = (bf16[4096,128]{1,0:T(8,128)(2,1)S(1)}, bf16[4096,128]{1,0:T(8,128)(2,1)}, u32[]{:S(2)}) copy-start(bf16[4096,128]{1,0:T(8,128)(2,1)} %param.13) | copy-start | bytes 3145732
  12.9 21.9 %all-to-all-start.1 = ((s32[8,1,64]{2,1,0:T(1,128)}), s32[8,1,64]{2,1,0:T(1,128)S(1)}, u32[]{:S(2)}, u32[]{:S(2)}) async-start(s32[8,1,64]{2,1,0:T(1,128)} %all_to_all.24), calls=%async_computation.1 | async-start | bytes 8192 | tf_op jit(solution)/shard_map/all_to_all | solution.py:48
  34.8 8.7 %all-to-all-start = ((s32[8,1,64]{2,1,0:T(1,128)}), s32[8,1,64]{2,1,0:T(1,128)S(1)}, u32[]{:S(2)}, u32[]{:S(2)}) async-start(s32[8,1,64]{2,1,0:T(1,128)} %all_to_all.22), calls=%async_computation | async-start | bytes 8192 | tf_op jit(solution)/shard_map/all_to_all | solution.py:49
  45.8 10.1 %all-to-all-start.2 = ((bf16[8,64,128]{2,1,0:T(8,128)(2,1)}), bf16[8,64,128]{2,1,0:T(8,128)(2,1)S(1)}, u32[]{:S(2)}, u32[]{:S(2)}) async-start(bf16[8,64,128]{2,1,0:T(8,128)(2,1)} %select_select_fusion), calls=%async_computation.2 | async-start | bytes 262144 | tf_op jit(solution)/shard_map/all_to_all | solution.py:52
  49.2 54.3 %reduce-scatter.2.cloned.1.call-start = ((), (), s32[]{:S(2)}) async-start(), calls=%async_computation.5 | async-start | bytes 589824 | tf_op jit(solution)/shard_map/reduce_scatter | solution.py:72
  49.2 21.1 %copy-start.1 = (bf16[256,512]{1,0:T(8,128)(2,1)S(1)}, bf16[256,512]{1,0:T(8,128)(2,1)}, u32[]{:S(2)}) copy-start(bf16[256,512]{1,0:T(8,128)(2,1)} %param.14) | copy-start | bytes 786436
  105.4 10.1 %all-to-all-start.3 = ((bf16[8,64,128]{2,1,0:T(8,128)(2,1)}), bf16[8,64,128]{2,1,0:T(8,128)(2,1)S(1)}, u32[]{:S(2)}, u32[]{:S(2)}) async-start(bf16[8,64,128]{2,1,0:T(8,128)(2,1)} %bitcast.27), calls=%async_computation.4 | async-start | bytes 262144 | tf_op jit(solution)/shard_map/all_to_all | solution.py:87
  108.8 95.1 %all-reduce.4.cloned.1.call-start = ((), (), s32[]{:S(2)}) async-start(), calls=%async_computation.6 | async-start | bytes 2621440 | tf_op jit(solution)/shard_map/psum | solution.py:93
  115.5 3.4 %copy-start.3 = (bf16[1,512]{1,0:T(2,128)(2,1)S(1)}, bf16[1,512]{1,0:T(2,128)(2,1)}, u32[]{:S(2)}) copy-start(bf16[1,512]{1,0:T(2,128)(2,1)} %param.16) | copy-start | bytes 3076
  118.9 17.3 %copy-start.2 = (bf16[128,256]{1,0:T(8,128)(2,1)S(1)}, bf16[128,256]{1,0:T(8,128)(2,1)}, u32[]{:S(2)}) copy-start(bf16[128,256]{1,0:T(8,128)(2,1)} %reduce-scatter.2.cloned.1.call-done) | copy-start | bytes 196612
Sparse Core Ops, SparseCore 0:
  74.0 29.4 reduce-scatter.1
  119.0 61.0 all-reduce.3
where the time goes:
time: 216 us; the launch traced here: 215 us
  blocking collectives  104 us (48%)
  waiting for transfers between devices  42.6 us (20%)
  matrix products  17.9 us (8%)
  starting transfers between devices  16.5 us (8%)
  between operations  14.2 us (7%)
  local copies, waits for them, and re-layouts  10.1 us (5%)
  other arithmetic  9.09 us (4%)
    psum x1, blocking collectives, shards(): hot_everywhere = lax.psum(hot_part, ('dp', 'shard'))  63.7 us
    reduce_scatter x1, waiting for transfers between devices, shards(): lax.psum_scatter(jnp.dot(hidden_grad, w_in.T, preferred_element_type=jnp....  28.9 us
    psum x1, blocking collectives, shards(): group_logits = lax.psum(logit_share, 'shard')  14.4 us
    all_gather x1, blocking collectives, shards(): group_inputs = lax.all_gather(inputs, 'shard', axis=0, tiled=True)  14 us
    all_gather x1, blocking collectives, shards(): group_cotangent = lax.all_gather(cotangent, 'shard', axis=0, tiled=True)  12.3 us
    dot_general x4, matrix products, contract_rows(): lax.dot_general(left, right, (((0,), (0,)), ((), ())), preferred_element_...  8.01 us
    all_to_all x1, starting transfers between devices, shards(): lax.all_to_all(requests, 'shard', split_axis=0, concat_axis=0, tiled=True)  6.33 us
    all_to_all x1, waiting for transfers between devices, shards(): lax.all_to_all(outgoing, 'shard', split_axis=0, concat_axis=0, tiled=True)  5.5 us
  transfers between devices with their start and end apart: 6, of which 4 were waited for; matrix products, arithmetic and copies ran while one was open for 7% of the time, Pallas kernels for 0%

commit v1 on v0

--- a/solution.py
+++ b/solution.py
@@ -76,7 +76,7 @@
         tiled=True,
     )
     hot_part = contract_rows(hot_counts, input_grad[:, :embed])
-    hot_everywhere = lax.psum(hot_part, ("dp", "shard"))
+    hot_everywhere = lax.psum(lax.psum(hot_part, "shard"), "dp")
     hot_total = lax.dynamic_slice_in_dim(hot_everywhere, my_index * kept_rows, kept_rows, 0)
     per_lookup = jnp.repeat(input_grad[:, embed:], per_sample, axis=0)
     outgoing = (

time: 216 us -> 280 us (1.30)
  waiting for transfers between devices: 42.6 us -> 75.4 us
  blocking collectives: 104 us -> 135 us
    psum x0 -> x1, waiting for transfers between devices: none -> 30.7 us  [shards(): hot_everywhere = lax.psum(lax.psum(hot_part, 'shard'), 'dp')]
    psum x1, blocking collectives: 63.7 us -> 94.2 us  [shards(): hot_everywhere = lax.psum(lax.psum(hot_part, 'shard'), 'dp')]
  transfers between devices with their start and end apart: 6 -> 7, of which waited for: 4 -> 5; matrix products, arithmetic and copies ran while one was open for 7% -> 6% of each run, Pallas kernels for 0% -> 0%
where the time goes in v1:
time: 280 us; the launch traced here: 279 us
  blocking collectives  135 us (48%)
  waiting for transfers between devices  75.4 us (27%)
  matrix products  19.9 us (7%)
  starting transfers between devices  16.7 us (6%)
  between operations  13.9 us (5%)
  other arithmetic  9.09 us (3%)
  local copies, waits for them, and re-layouts  8.44 us (3%)
    psum x1, blocking collectives, shards(): hot_everywhere = lax.psum(lax.psum(hot_part, 'shard'), 'dp')  94.2 us
    psum x1, waiting for transfers between devices, shards(): hot_everywhere = lax.psum(lax.psum(hot_part, 'shard'), 'dp')  30.7 us
    reduce_scatter x1, waiting for transfers between devices, shards(): lax.psum_scatter(jnp.dot(hidden_grad, w_in.T, preferred_element_type=jnp....  29.6 us
    psum x1, blocking collectives, shards(): group_logits = lax.psum(logit_share, 'shard')  14.8 us
    all_gather x1, blocking collectives, shards(): group_inputs = lax.all_gather(inputs, 'shard', axis=0, tiled=True)  14 us
    all_gather x1, blocking collectives, shards(): group_cotangent = lax.all_gather(cotangent, 'shard', axis=0, tiled=True)  12.3 us
    dot_general x4, matrix products, contract_rows(): lax.dot_general(left, right, (((0,), (0,)), ((), ())), preferred_element_...  10.1 us
    all_to_all x1, waiting for transfers between devices, shards(): lax.all_to_all(outgoing, 'shard', split_axis=0, concat_axis=0, tiled=True)  6.9 us
  transfers between devices with their start and end apart: 7, of which 5 were waited for; matrix products, arithmetic and copies ran while one was open for 6% of the time, Pallas kernels for 0%

profile of v1, /device:TPU:0, one launch (start us, length us, event | category | flops | bytes accessed | tf_op | source)
XLA Modules:
  0.0 278.6 jit_solution(12758000550311607130)
XLA Ops:
  7.2 0.0 copy-start
  7.2 0.8 fusion.11
  8.0 0.6 reduce-window.6
  8.5 0.2 slice_reduce_fusion
  8.8 0.8 fusion.10
  9.6 0.5 broadcast.99
  10.1 1.3 fusion.14
  11.4 0.8 convert_reduce_fusion
  12.3 0.7 all_to_all.24
  12.9 6.3 %all-to-all-start.1 = ((s32[8,1,64]{2,1,0:T(1,128)}), s32[8,1,64]{2,1,0:T(1,128)S(1)}, u32[]{:S(2)}, u32[]{:S(2)}) async-start(s32[8,1,64]{2,1,0:T(1,128)} %all_to_all.24), calls=%async_computation.1 | async-start | bytes 8192 | tf_op jit(solution)/shard_map/all_to_all | solution.py:48
  19.3 1.0 slice_bitcast_fusion.7
  20.2 0.7 reduce.2
  20.9 0.7 add.106
  21.6 0.7 all_to_all.22
  22.3 0.1 eq.239
  22.4 0.1 copy.20
  22.5 12.3 %all-gather = f32[8,1,128]{2,1,0:T(1,128)S(1)} all-gather(f32[1,1,128]{2,1,0:T(1,128)} %bitcast.77), channel_id=1, replica_groups=mesh['dp'=4,'shard'=8] {'shard'}, dimensions={0}, use_global_device_ids=true | all-gather | bytes 4608 | tf_op jit(solution)/shard_map/all_gather | solution.py:66
  34.8 0.0 all-to-all-done.1
  34.8 3.3 %all-to-all-start = ((s32[8,1,64]{2,1,0:T(1,128)}), s32[8,1,64]{2,1,0:T(1,128)S(1)}, u32[]{:S(2)}, u32[]{:S(2)}) async-start(s32[8,1,64]{2,1,0:T(1,128)} %all_to_all.22), calls=%async_computation | async-start | bytes 8192 | tf_op jit(solution)/shard_map/all_to_all | solution.py:49
  38.2 0.1 reshape.125
  38.3 5.3 %all-to-all-done = s32[8,1,64]{2,1,0:T(1,128)S(1)} async-done(((s32[8,1,64]{2,1,0:T(1,128)}), s32[8,1,64]{2,1,0:T(1,128)S(1)}, u32[]{:S(2)}, u32[]{:S(2)}) %all-to-all-start) | async-done | bytes 2080 | tf_op jit(solution)/shard_map/all_to_all | solution.py:49
  43.6 0.0 copy-done
  43.6 1.3 gather_fusion
  44.9 0.9 select_select_fusion
  45.8 3.4 %all-to-all-start.2 = ((bf16[8,64,128]{2,1,0:T(8,128)(2,1)}), bf16[8,64,128]{2,1,0:T(8,128)(2,1)S(1)}, u32[]{:S(2)}, u32[]{:S(2)}) async-start(bf16[8,64,128]{2,1,0:T(8,128)(2,1)} %select_select_fusion), calls=%async_computation.2 | async-start | bytes 262144 | tf_op jit(solution)/shard_map/all_to_all | solution.py:52
  49.2 0.0 reduce-scatter.2.cloned.1.call-start
  49.2 0.0 copy-start.1
  49.2 3.7 %convolution_convert_fusion.3 = bf16[128,128]{0,1:T(8,128)(2,1)S(1)} fusion(bf16[4096,128]{1,0:T(8,128)(2,1)} %param.12, s32[128]{0:T(128)S(1)} %get-tuple-element.16, s32[128]{0:T(128)S(1)} %get-tuple-element.17, s32[128]{0:T(128)S(1)} %get-tuple-element.11, s32[128]{0:T(128)S(1)} %get-tuple-element.12, s32[128]{0:T(128)S(1)} %get-tuple-element.13, ...), kind=kOutput, calls=%fused_computation.21 | convolution fusion | flops 146817024 | bytes 1085440 | tf_op jit(solution)/shard_map/dot_general | solution.py:31
  53.0 2.9 %all-to-all-done.2 = bf16[8,64,128]{2,1,0:T(8,128)(2,1)S(1)} async-done(((bf16[8,64,128]{2,1,0:T(8,128)(2,1)}), bf16[8,64,128]{2,1,0:T(8,128)(2,1)S(1)}, u32[]{:S(2)}, u32[]{:S(2)}) %all-to-all-start.2) | async-done | bytes 131104 | tf_op jit(solution)/shard_map/all_to_all | solution.py:52
  55.9 0.3 convolution_reduce_fusion
  56.1 0.1 copy.22
  56.3 14.0 %all_gather.6 = bf16[1024,256]{0,1:T(8,128)(2,1)S(1)} all-gather(bf16[128,256]{0,1:T(8,128)(2,1)S(1)} %pad_maximum_fusion), channel_id=1, replica_groups=mesh['dp'=4,'shard'=8] {'shard'}, dimensions={0}, use_global_device_ids=true | all-gather | bytes 589824 | tf_op jit(solution)/shard_map/all_gather | solution.py:56
  70.3 0.0 copy-done.1
  70.3 2.3 multiply_convert_fusion
  72.6 1.3 convolution_convert_fusion
  73.8 0.0 reduce-scatter.2.cloned.1.call-update
  73.8 0.0 all-reduce.5.cloned.1.call-start
  73.9 29.6 %reduce-scatter.2.cloned.1.call-done = bf16[128,256]{1,0:T(8,128)(2,1)} async-done(((bf16[1024,256]{1,0:T(8,128)(2,1)}), bf16[128,256]{1,0:T(8,128)(2,1)}) %reduce-scatter.2.cloned.1.call-update) | async-done | bytes 65552 | tf_op jit(solution)/shard_map/reduce_scatter | solution.py:72
  103.5 4.4 %fusion.6 = f32[4096,128]{1,0:T(8,128)} fusion(s32[128]{0:T(128)S(1)} %get-tuple-element.16, s32[128]{0:T(128)S(1)} %get-tuple-element.17, s32[128]{0:T(128)S(1)} %get-tuple-element.11, s32[128]{0:T(128)S(1)} %get-tuple-element.12, s32[128]{0:T(128)S(1)} %get-tuple-element.13, s32[128]{0:T(128)S(1)} %get-tuple-element.14, s32[128]{0:T(128)S(1)} %get-tuple-element.15, ...), kind=kOutput, calls=%fused_computation.28 | convolution fusion | flops 146800640 | bytes 2134016 | tf_op jit(solution)/shard_map/dot_general | solution.py:8
  107.9 0.0 slice-start
  107.9 0.0 all-reduce.5.cloned.1.call-update
  107.9 0.7 reduce.10
  108.6 0.1 eq.248
  108.7 0.0 slice-done
  108.7 1.1 convolution_convert_fusion.2
  109.8 3.4 %all-to-all-start.3 = ((bf16[8,64,128]{2,1,0:T(8,128)(2,1)}), bf16[8,64,128]{2,1,0:T(8,128)(2,1)S(1)}, u32[]{:S(2)}, u32[]{:S(2)}) async-start(bf16[8,64,128]{2,1,0:T(8,128)(2,1)} %bitcast.27), calls=%async_computation.4 | async-start | bytes 262144 | tf_op jit(solution)/shard_map/all_to_all | solution.py:87
  113.2 0.2 all-reduce.7.cloned.1.call-start
  113.4 1.1 convolution_convert_fusion.1
  114.5 6.9 %all-to-all-done.3 = bf16[8,64,128]{2,1,0:T(8,128)(2,1)S(1)} async-done(((bf16[8,64,128]{2,1,0:T(8,128)(2,1)}), bf16[8,64,128]{2,1,0:T(8,128)(2,1)S(1)}, u32[]{:S(2)}, u32[]{:S(2)}) %all-to-all-start.3) | async-done | bytes 131104 | tf_op jit(solution)/shard_map/all_to_all | solution.py:87
  121.4 0.0 copy-start.2
  121.4 3.4 %fusion.1 = bf16[4096,128]{1,0:T(8,128)(2,1)} fusion(bf16[512,128]{1,0:T(8,128)(2,1)S(1)} %bitcast.62, s32[512]{0:T(512)S(1)} %eq.248), kind=kOutput, calls=%fused_computation.3 | convolution fusion | flops 539492352 | bytes 1181696 | tf_op jit(solution)/shard_map/dot_general | solution.py:8
  124.9 0.0 all-reduce.7.cloned.1.call-update
  124.9 0.0 copy-done.2
  124.9 2.3 fusion.3
  127.2 14.8 %psum.35 = f32[1024]{0:T(1024)S(1)} all-reduce(f32[1024]{0:T(1024)S(1)} %bitcast.71), channel_id=1, replica_groups=mesh['dp'=4,'shard'=8] {'shard'}, use_global_device_ids=true, to_apply=%region_6.7 | all-reduce | flops 1024 | bytes 8192 | tf_op jit(solution)/shard_map/psum | solution.py:64
  141.9 0.6 dynamic_slice.6
  142.5 30.7 %all-reduce.5.cloned.1.call-done = f32[4096,128]{1,0:T(8,128)} async-done(((f32[4096,128]{1,0:T(8,128)}), f32[4096,128]{1,0:T(8,128)}) %all-reduce.5.cloned.1.call-update) | async-done | bytes 2097168 | tf_op jit(solution)/shard_map/psum | solution.py:79
  173.2 94.2 %all-reduce.8 = bf16[4096,128]{1,0:T(8,128)(2,1)S(1)} all-reduce(f32[4096,128]{1,0:T(8,128)} %all-reduce.5.cloned.1.call-done), channel_id=1, replica_groups=mesh['dp'=4,'shard'=8] {'dp'}, use_global_device_ids=true, to_apply=%region_9.10 | all-reduce | flops 524288 | bytes 3145728 | tf_op jit(solution)/shard_map/psum | solution.py:79
  267.4 0.7 dynamic-slice_convert_fusion
  268.1 0.0 all-reduce.7.cloned.1.call-done
  268.1 1.8 convert_element_type.86
  269.9 2.3 copy.28
  (9 shorter events, 0.1 us)
Async XLA Ops:
  7.2 36.4 %copy-start = (bf16[4096,128]{1,0:T(8,128)(2,1)S(1)}, bf16[4096,128]{1,0:T(8,128)(2,1)}, u32[]{:S(2)}) copy-start(bf16[4096,128]{1,0:T(8,128)(2,1)} %param.13) | copy-start | bytes 3145732
  12.9 21.9 %all-to-all-start.1 = ((s32[8,1,64]{2,1,0:T(1,128)}), s32[8,1,64]{2,1,0:T(1,128)S(1)}, u32[]{:S(2)}, u32[]{:S(2)}) async-start(s32[8,1,64]{2,1,0:T(1,128)} %all_to_all.24), calls=%async_computation.1 | async-start | bytes 8192 | tf_op jit(solution)/shard_map/all_to_all | solution.py:48
  34.8 8.7 %all-to-all-start = ((s32[8,1,64]{2,1,0:T(1,128)}), s32[8,1,64]{2,1,0:T(1,128)S(1)}, u32[]{:S(2)}, u32[]{:S(2)}) async-start(s32[8,1,64]{2,1,0:T(1,128)} %all_to_all.22), calls=%async_computation | async-start | bytes 8192 | tf_op jit(solution)/shard_map/all_to_all | solution.py:49
  45.8 10.1 %all-to-all-start.2 = ((bf16[8,64,128]{2,1,0:T(8,128)(2,1)}), bf16[8,64,128]{2,1,0:T(8,128)(2,1)S(1)}, u32[]{:S(2)}, u32[]{:S(2)}) async-start(bf16[8,64,128]{2,1,0:T(8,128)(2,1)} %select_select_fusion), calls=%async_computation.2 | async-start | bytes 262144 | tf_op jit(solution)/shard_map/all_to_all | solution.py:52
  49.2 54.3 %reduce-scatter.2.cloned.1.call-start = ((), (), s32[]{:S(2)}) async-start(), calls=%async_computation.5 | async-start | bytes 589824 | tf_op jit(solution)/shard_map/reduce_scatter | solution.py:72
  49.2 21.1 %copy-start.1 = (bf16[256,512]{1,0:T(8,128)(2,1)S(1)}, bf16[256,512]{1,0:T(8,128)(2,1)}, u32[]{:S(2)}) copy-start(bf16[256,512]{1,0:T(8,128)(2,1)} %param.14) | copy-start | bytes 786436
  73.8 99.3 %all-reduce.5.cloned.1.call-start = ((), (), s32[]{:S(2)}) async-start(), calls=%async_computation.6 | async-start | bytes 4194304 | tf_op jit(solution)/shard_map/psum | solution.py:79
  107.9 0.8 slice-start
  109.8 11.7 %all-to-all-start.3 = ((bf16[8,64,128]{2,1,0:T(8,128)(2,1)}), bf16[8,64,128]{2,1,0:T(8,128)(2,1)S(1)}, u32[]{:S(2)}, u32[]{:S(2)}) async-start(bf16[8,64,128]{2,1,0:T(8,128)(2,1)} %bitcast.27), calls=%async_computation.4 | async-start | bytes 262144 | tf_op jit(solution)/shard_map/all_to_all | solution.py:87
  113.2 154.9 %all-reduce.7.cloned.1.call-start = ((), (), s32[]{:S(2)}) async-start(), calls=%async_computation.7 | async-start | bytes 2621440 | tf_op jit(solution)/shard_map/psum | solution.py:93
  121.4 3.4 %copy-start.2 = (bf16[1,512]{1,0:T(2,128)(2,1)S(1)}, bf16[1,512]{1,0:T(2,128)(2,1)}, u32[]{:S(2)}) copy-start(bf16[1,512]{1,0:T(2,128)(2,1)} %param.16) | copy-start | bytes 3076
Sparse Core Ops, SparseCore 0:
  74.0 29.4 reduce-scatter.1
  108.0 65.1 all-reduce.4
  177.2 77.7 all-reduce.6
